TPU v7x, 32 devices: a whole 2x2x4 slice. The times are simulated.
32 devices in a mesh: gx: 16 (over z, y, x), gy: 2 (over core).
Axes of the slice: x: 2, y: 2, z: 4, core: 2. Of those that a mesh axis runs over, the one named last changes fastest.
Arguments:
- velocity: float32 [512, 64, 128], P('gx', 'gy'), may hold values from -6 to 6
Outputs:
- coefficients: float32 [512, 64, 128], P('gx', 'gy')
All inputs are finite; a program needn't handle non-finite values.
Results may differ from a plain program's by a relative error of at most 0.00002.
Values sent between devices are 32-bit elements; how exact they have to be, the bound alone decides.
No kernel may reach another device: no remote copies, remote signals or barrier semaphores. Data moves between devices by JAX's collectives and lax.ppermute only.
A program may use at most 128 MiB of HBM per device.

v0:
```python
import functools

import jax
import jax.numpy as jnp
import numpy as np
from jax import lax
from jax.experimental import pallas as pl
from jax.experimental.pallas import tpu as pltpu
from jax.sharding import PartitionSpec as P

LEVELS = 4
STEPS = (-1.586134342, -0.05298011854, 0.8829110762, 0.4435068522)
SCALE = 1.149604398
VMEM_BYTES = 24 * 2**20
FIRST_FLOPS = 10**10
COPIES = 2
SHARED = False


def windows(block):
    found = []
    first, last = 0, block - 1
    for _ in range(LEVELS):
        low = first - 4 + (first % 2)
        high = last + 4 - (last % 2)
        found.append((low, high))
        first, last = low // 2, high // 2
    return found


def message(block, rows, to):
    sent, derived = {}, {}
    spans = windows(block)
    base = ends = 0
    for level, (low, high) in enumerate(spans):
        size, height = block >> level, rows >> level
        first, last = (0, block - 1) if level == 0 else (v // 2 for v in spans[level - 1])
        planes = [p for p in range(low, high + 1) if p // size == to]
        if abs(to) == 1:
            sign = to
            edge = last + 2 - last % 2 if to > 0 else first - 2 + first % 2
            far, near = edge + sign, edge - sign
            if far in planes and edge + 2 * sign in planes:
                derived[level, edge + 2 * sign] = (far, None)
            if far in planes and near in planes:
                derived[level, edge] = (far, near)
        at = base
        for plane in planes:
            if (level, plane) not in derived:
                sent[level, plane] = at
                at += height
        ends = max(ends, at)
        if level == 0:
            base = at
    return sent, derived, -(-ends // 8) * 8


def shift_of(level):
    return (0, 0, 1, 3)[level]


def places_of(block):
    found = set()
    for level, (low, high) in enumerate(windows(block)):
        size = block >> level
        found |= set(range(low // size, high // size + 1))
    return sorted(found - {0})


def z_product(value, weights):
    width = value.shape[-1]
    high = value.astype(jnp.bfloat16)
    rest = (value - high.astype(jnp.float32)).astype(jnp.bfloat16)
    both = jnp.concatenate([high, rest], axis=1)
    product = jnp.dot(both, weights, preferred_element_type=jnp.float32)
    return product[:, :width] + product[:, width:]


def lanes_of(width, spacing, parity):
    lane = lax.broadcasted_iota(jnp.int32, (1, width), 1)
    return lax.rem(lane, 2 * spacing) == (spacing if parity else 0)


def own_lanes(width, level, high_only):
    spacing, shift = 1 << level, shift_of(level)
    lane = lax.broadcasted_iota(jnp.int32, (1, width), 1)
    if high_only:
        return lax.rem(lane, 2 * spacing) == spacing + shift
    return lax.rem(lane, spacing) == shift


def z_lift(value, spacing):
    width = value.shape[-1]
    axis = value.ndim - 1
    for step, weight in enumerate(STEPS):
        factor = jnp.where(lanes_of(width, spacing, step % 2 == 0), weight, 0.0)
        around = pltpu.roll(value, spacing, axis) + pltpu.roll(value, width - spacing, axis)
        value = value + factor * around
    return value


def x_lift(planes):
    def plus(one, other):
        return other if one is None else one if other is None else one + other

    planes = dict(planes)
    for step, weight in enumerate(STEPS):
        parity = 1 if step % 2 == 0 else 0
        for index in range(min(planes) - 1, max(planes) + 2):
            if index % 2 == parity:
                around = plus(planes.get(index - 1), planes.get(index + 1))
                if around is not None:
                    planes[index] = plus(planes.get(index), weight * around)
    return planes


def y_lift_split(even, odd):
    count = even.shape[0]
    a, b, c, d = STEPS
    odd = odd + a * (even + pltpu.roll(even, count - 1, 0))
    even = even + b * (pltpu.roll(odd, 1, 0) + odd)
    odd = odd + c * (even + pltpu.roll(even, count - 1, 0))
    even = even + d * (pltpu.roll(odd, 1, 0) + odd)
    return even, odd


def y_lift_whole(value):
    count = value.shape[0]
    row = lax.broadcasted_iota(jnp.int32, (count, 1), 0)
    for step, weight in enumerate(STEPS):
        factor = jnp.where(lax.rem(row, 2) == (1 if step % 2 == 0 else 0), weight, 0.0)
        value = value + factor * (pltpu.roll(value, 1, 0) + pltpu.roll(value, count - 1, 0))
    return value


def scaled_z(value, spacing):
    width = value.shape[-1]
    odd, even = lanes_of(width, spacing, True), lanes_of(width, spacing, False)
    return value * jnp.where(odd, SCALE, jnp.where(even, 1 / SCALE, 0.0))


def scaled(value, x_odd, y_odd):
    at = (SCALE if x_odd else 1 / SCALE) * (SCALE if y_odd else 1 / SCALE)
    return value if x_odd != y_odd else value * at


def spread_z(source, weights, spread, rows, start, size):
    width = source.shape[-1]
    value = source[start : start + size].reshape(size * rows, width)
    spread[start * rows : (start + size) * rows, :] = z_product(value, weights[...])


def spread_x(block, rows, spread, into, low, base):
    for at in range(0, rows, 8):
        planes = {x: spread[x * rows + at : x * rows + at + 8, :] for x in range(block)}
        for x, value in x_lift(planes).items():
            into[x - low, base + at : base + at + 8, :] = value


def matrix_kernel(*weights):
    width = weights[0].shape[0] // 2
    row = lax.broadcasted_iota(jnp.int32, (width, width), 0)
    lane = lax.broadcasted_iota(jnp.int32, (width, width), 1)
    value = jnp.where(row == lane, 1.0, 0.0)
    full = [scaled_z(z_lift(value, 1), 1), jnp.zeros((width, width), jnp.float32)]
    for level in range(1, LEVELS):
        spacing = 1 << level
        value = scaled_z(z_lift(value, spacing), spacing)
        full[1] += pltpu.roll(value, shift_of(level), 1) if shift_of(level) else value
        value = jnp.where(lanes_of(width, spacing, False), value, 0.0)
    for weight, matrix in zip(weights, full):
        high = matrix.astype(jnp.bfloat16)
        rest = (matrix - high.astype(jnp.float32)).astype(jnp.bfloat16)
        weight[:width, :width] = high
        weight[:width, width:] = rest
        weight[width:, :width] = high
        weight[width:, width:] = jnp.zeros_like(rest)


def own_kernel(block, rows, velocity, weights, into, spread):
    step = max(1, min(block, 512 // rows))
    for x in range(0, block, step):
        spread_z(velocity, weights, spread, rows, x, step)
    spread_x(block, rows, spread, into, windows(block)[0][0], 0)


def message_kernel(block, rows, width, count, places, *refs):
    refs = list(refs)

    def take(number):
        taken = refs[:number]
        del refs[:number]
        return taken

    shared = count == 2 and SHARED
    halves = 2 if shared else 1
    (_,) = take(1)
    others = take(count - 1)
    weights = take(2)
    (first,) = take(1)
    own = take(LEVELS)
    passed = take(2 if shared else len(places))
    (spread,) = take(1)
    lifted = [first] + take(LEVELS - 1)
    coarse = take(LEVELS - 1)
    messages = dict(zip(places, take(len(places)) if shared else passed))
    spans = windows(block)
    total = count * rows
    tables = {to: message(block, rows, to) for to in places}
    lengths = {to: messages[to].shape[0] // halves for to in places}
    written = {to: set() for to in places}

    def post(to, at, number, value):
        here = range(at, at + 2 * number, 2)
        if written[to].isdisjoint(here):
            messages[to][pl.ds(at, number, 2), :] = value
        else:
            messages[to][pl.ds(at, number, 2), :] += value
        written[to].update(here)

    def put(level, plane, half, even, odd):
        number = (rows >> level) // 2
        low = level < LEVELS - 1 and plane % 2 == 0
        if level > 0 or low:
            even = jnp.where(own_lanes(width, level, low), even, 0.0)
        if level > 0:
            odd = jnp.where(own_lanes(width, level, False), odd, 0.0)
        to = plane // (block >> level)
        if to == 0:
            own[level][plane, pl.ds(0, number, 2), :] = even
            own[level][plane, pl.ds(1, number, 2), :] = odd
        else:
            at = tables[to][0][level, plane] + half * lengths[to]
            post(to, at, number, even)
            post(to, at + 1, number, odd)

    for level in range(LEVELS):
        low, high = spans[level]
        height = total >> level
        half, mine = height // 2, (rows >> level) // 2
        into = lifted[level]

        if level == 0:
            for part, source in enumerate(others):
                step = min(block, max(1, 512 // rows))
                for x in range(0, block, step):
                    spread_z(source, weights[0], spread, rows, x, step)
                spread_x(block, rows, spread, into, low, (part + 1) * rows)
        else:
            start, stop = spans[level - 1][0] // 2, spans[level - 1][1] // 2 + 1
            source = coarse[level - 1]
            if level == 1:
                size = (stop - start) * height
                for at in range(0, size, 512):
                    end = min(size, at + 512)
                    source[at:end, :] = z_product(source[at:end, :], weights[level][...])
            for at in range(0, height, 8):
                planes = {}
                for x in range(start, stop):
                    row = (x - start) * height + at
                    planes[x] = source[row : row + 8, :]
                for x, value in x_lift(planes).items():
                    into[x - low, at : at + 8, :] = value

        for plane in range(low, high + 1):
            odd_plane = plane % 2 == 1
            to = plane // (block >> level)
            if level == 0 and odd_plane and to == 0:
                continue
            goes_on = level < LEVELS - 1 and not odd_plane
            sends = to == 0 or (level, plane) in tables[to][0]
            if not goes_on and not sends:
                continue
            at = plane - low
            split = half % 8 == 0
            if split:
                even, odd = y_lift_split(
                    into[at, pl.ds(0, half, 2), :], into[at, pl.ds(1, half, 2), :]
                )
                even = scaled(even, odd_plane, False)
            else:
                into[at] = y_lift_whole(into[at])
                even = scaled(into[at, pl.ds(0, half, 2), :], odd_plane, False)
            if goes_on:
                row = ((plane - low) // 2) * half
                coarse[level][row : row + half, :] = even
            if not sends:
                continue
            for part in range(halves if to else 1):
                if split:
                    here_even = even[part * mine : (part + 1) * mine]
                    here_odd = odd[part * mine : (part + 1) * mine]
                else:
                    here_even = into[at, pl.ds(2 * part * mine, mine, 2), :]
                    here_even = scaled(here_even, odd_plane, False)
                    here_odd = into[at, pl.ds(2 * part * mine + 1, mine, 2), :]
                put(level, plane, part, here_even, scaled(here_odd, odd_plane, True))

    for to in places:
        for row in range(halves * lengths[to]):
            if row not in written[to]:
                messages[to][row : row + 1, :] = jnp.zeros((1, width), jnp.float32)
    if shared:
        for far, target in enumerate(passed, 1):
            target[...] = jnp.where(lax.axis_index("gy") == 0, messages[-far][...], messages[far][...])


def rest_kernel(block, rows, width, first, _, *refs):
    coarse, out = refs[:-1], refs[-1]
    low = windows(block)[0][0]
    half, mine = first.shape[1] // 2, rows // 2
    for plane in range(1, block, 2):
        even, odd = y_lift_split(
            first[plane - low, pl.ds(0, half, 2), :], first[plane - low, pl.ds(1, half, 2), :]
        )
        out[plane, pl.ds(0, mine, 2), :] = scaled(even[:mine], True, False)
        out[plane, pl.ds(1, mine, 2), :] = scaled(odd[:mine], True, True)
    for level in range(1, LEVELS):
        spacing, shift = 1 << level, shift_of(level)
        for plane in range(block >> level):
            value = coarse[level - 1][plane]
            if shift:
                value = pltpu.roll(value, width - shift, 1)
            out[plane * spacing, pl.ds(0, rows >> level, spacing), :] += value


def add_message(block, rows, to, arrived, base, out, clean):
    sent, derived, _ = message(block, rows, to)
    a, b, c, d = STEPS
    width = out.shape[-1]
    for level in sorted({level for level, _ in sent}):
        spacing, height = 1 << level, rows >> level
        shape = (height, width)
        if level > 0:
            here = [at for (found, _), at in sent.items() if found == level]
            start, stop = min(here), -(-(max(here) + height) // 8) * 8
            value = arrived[base + start : base + stop, :]
            if shift_of(level):
                value = pltpu.roll(value, width - shift_of(level), 1)
            lane = lax.broadcasted_iota(jnp.int32, (1, width), 1)
            value = jnp.where(lax.rem(lane, spacing) == 0, value, 0.0)
            source = clean[level - 1]
            source[: stop - start, :] = value
        else:
            start, source = -base, arrived

        def read(plane):
            at = sent[level, plane] - start
            return source[at : at + height, :]

        def add(plane, value):
            x = (plane - to * (block >> level)) * spacing
            out[x, pl.ds(0, height, spacing), :] += value

        for found, plane in sent:
            if found == level:
                add(plane, read(plane))
        for (found, plane), (far, near) in derived.items():
            if found == level:
                if near is None:
                    value = (d / SCALE**2) * read(far)
                else:
                    value = ((1 / c + d) / SCALE**2) * read(far) + (d / SCALE**2) * read(near)
                row = lax.broadcasted_iota(jnp.int32, shape, 0)
                keep = (lax.rem(row, 2) == 1) | lanes_of(width, spacing, True)
                add(plane, jnp.where(keep, value, 0.0))


def write_out(out, whole, done):
    parts = done.shape[0]
    size = out.shape[0] // parts
    copies = [
        pltpu.make_async_copy(
            out.at[pl.ds(part * size, size)], whole.at[pl.ds(part * size, size)], done.at[part]
        )
        for part in range(parts)
    ]
    for copy in copies:
        copy.start()
    for copy in copies:
        copy.wait()


def add_kernel(block, rows, places, last, _, *refs):
    received, refs = refs[: len(places)], refs[len(places) :]
    if last:
        whole, out, done, *clean = refs
    else:
        out, *clean = refs
    for to, arrived in zip(places, received):
        add_message(block, rows, to, arrived, 0, out, clean)
    if last:
        write_out(out, whole, done)


def keep_kernel(block, rows, _, near, far, out, *clean):
    for core, side in enumerate((-1, 1)):

        @pl.when(lax.axis_index("gy") == core)
        def _():
            add_message(block, rows, side, near, 0, out, clean)
            add_message(block, rows, 2 * side, far, 0, out, clean)


def pack_kernel(near, far, packed):
    one, two = near.shape[0] // 2, far.shape[0] // 2
    packed[:one, :] = near[one:, :]
    packed[one:, :] = far[two:, :]


def swap_kernel(block, rows, one, _, packed, whole, out, done, *clean):
    for core, side in enumerate((1, -1)):

        @pl.when(lax.axis_index("gy") == core)
        def _():
            add_message(block, rows, side, packed, 0, out, clean)
            add_message(block, rows, 2 * side, packed, one, out, clean)

    write_out(out, whole, done)


def call(body, name, outs, ins, scratch=(), aliases=None, flops=0, hbm_out=()):
    vmem, hbm = pl.BlockSpec(memory_space=pltpu.VMEM), pl.BlockSpec(memory_space=pltpu.HBM)
    f32 = jnp.float32
    shapes = [out if isinstance(out, jax.ShapeDtypeStruct) else jax.ShapeDtypeStruct(out, f32) for out in outs]
    moved = 4 * sum(int(np.prod(shape.shape)) for shape in shapes)
    return pl.pallas_call(
        body,
        out_shape=shapes,
        in_specs=[vmem] * len(ins),
        out_specs=[hbm if n in hbm_out else vmem for n in range(len(outs))],
        scratch_shapes=[pltpu.VMEM(shape, f32) if isinstance(shape, tuple) else shape for shape in scratch],
        input_output_aliases=aliases or {},
        compiler_params=pltpu.CompilerParams(vmem_limit_bytes=VMEM_BYTES),
        cost_estimate=pl.CostEstimate(flops=flops, bytes_accessed=2 * moved, transcendentals=0),
        name=name,
    )(*ins)


def local(velocity):
    block, rows, width = velocity.shape
    around, count = lax.axis_size("gx"), lax.axis_size("gy")
    shared = count == 2 and SHARED
    places = places_of(block)
    spans = windows(block)
    total = count * rows

    others = [
        lax.ppermute(velocity, "gy", [(i, (i - k) % count) for i in range(count)])
        for k in range(1, count)
    ]
    lifted = [
        (high - low + 1, total >> level, width) for level, (low, high) in enumerate(spans)
    ]
    coarse = [
        ((high // 2 - low // 2 + 1) * (total >> (level + 1)), width)
        for level, (low, high) in enumerate(spans[:-1])
    ]
    spread = (block * rows, width)
    owned = [(block >> level, rows >> level, width) for level in range(LEVELS)]
    lengths = {to: message(block, rows, to)[2] for to in places}
    one, two = max(lengths[1], lengths[-1]), max(lengths[2], lengths[-2])
    clean = [(one, width)] * (LEVELS - 1)

    square = jax.ShapeDtypeStruct((2 * width, 2 * width), jnp.bfloat16)
    weights = call(matrix_kernel, "make_matrices", [square] * 2, [], flops=FIRST_FLOPS)
    (first,) = call(
        functools.partial(own_kernel, block, rows),
        "lift_own",
        [lifted[0]],
        [velocity, weights[0]],
        [spread],
    )
    if shared:
        each = {to: (2 * (one if abs(to) == 1 else two), width) for to in places}
        outs, scratch = [each[1], each[2]], [each[to] for to in places]
    else:
        outs, scratch = [(lengths[to], width) for to in places], []
    first, kept, *more = call(
        functools.partial(message_kernel, block, rows, width, count, places),
        "make_messages",
        [lifted[0]] + owned + outs,
        [first] + others + list(weights),
        [spread] + lifted[1:] + coarse + scratch,
        {0: 0},
    )
    own_coarse, messages = more[: LEVELS - 1], more[LEVELS - 1 :]

    def rest():
        return call(
            functools.partial(rest_kernel, block, rows, width),
            "finish_own",
            [owned[0]],
            [first, kept] + own_coarse,
            aliases={1: 0},
        )[0]

    written = [pltpu.SemaphoreType.DMA((COPIES,))]
    if shared:
        near, far = (
            lax.ppermute(
                value,
                ("gx", "gy"),
                [
                    (2 * i + core, 2 * ((i + side * step) % around) + core)
                    for i in range(around)
                    for core, side in enumerate((-1, 1))
                ],
            )
            for step, value in enumerate(messages, 1)
        )
        result = rest()
        (packed,) = call(pack_kernel, "pack_other", [(one + two, width)], [near, far])
        packed = lax.ppermute(packed, "gy", [(0, 1), (1, 0)])
        (result,) = call(
            functools.partial(keep_kernel, block, rows),
            "add_kept",
            [owned[0]],
            [result, near, far],
            clean,
            aliases={0: 0},
        )
        whole, _ = call(
            functools.partial(swap_kernel, block, rows, one),
            "add_swapped",
            [owned[0]] * 2,
            [result, packed],
            written + clean,
            aliases={0: 1},
            hbm_out=(0,),
        )
        return whole

    sent = dict(zip(places, messages))
    received = {
        to: lax.ppermute(sent[to], "gx", [(i, (i + to) % around) for i in range(around)])
        for to in sorted(places, key=lambda to: (to < 0, abs(to)))
    }
    right = [to for to in places if to > 0]
    left = [to for to in places if to < 0]
    (result,) = call(
        functools.partial(add_kernel, block, rows, right, False),
        "add_right",
        [owned[0]],
        [rest()] + [received[to] for to in right],
        clean,
        aliases={0: 0},
        flops=FIRST_FLOPS,
    )
    whole, _ = call(
        functools.partial(add_kernel, block, rows, left, True),
        "add_left",
        [owned[0]] * 2,
        [result] + [received[to] for to in left],
        written + clean,
        aliases={0: 1},
        hbm_out=(0,),
    )
    return whole


def solution(mesh):
    return jax.shard_map(
        local, mesh=mesh, in_specs=(P("gx", "gy", None),), out_specs=P("gx", "gy", None), check_vma=False
    )
```

profile of v0, /device:TPU:0, one launch (start us, length us, event | category | flops | bytes accessed | tf_op | source)
XLA Modules:
  0.0 16.1 jit_solution(73350904312435902)
XLA Ops:
  0.0 0.0 copy-start
  0.0 0.5 %collective-permute-start = (f32[32,32,128]{2,1,0:T(8,128)}, f32[32,32,128]{2,1,0:T(8,128)S(1)}, u32[]{:S(2)}, u32[]{:S(2)}) collective-permute-start(f32[32,32,128]{2,1,0:T(8,128)} %velocity.1), channel_id=1, source_target_pairs={{0,1},{1,0},{2,3},{3,2},{4,5},{5,4},{6,7},{7,6},{8,9},{9,8},{10,11... | collective-permute-start | bytes 1572872 | tf_op jit(solution)/shard_map/ppermute | solution.py:449
  0.5 1.2 %make_matrices.1 = (bf16[256,256]{1,0:T(8,128)(2,1)S(1)}, bf16[256,256]{1,0:T(8,128)(2,1)S(1)}) custom-call(), custom_call_target="tpu_custom_call" | custom-call | flops 10000000000 | bytes 1048576 | tf_op jit(solution)/shard_map/make_matrices/pallas_call | solution.py:427
  1.6 0.0 copy-done
  1.7 0.3 %lift_own.1.refs_0_ = f32[39,64,128]{2,1,0:T(8,128)S(1)} custom-call(f32[32,32,128]{2,1,0:T(8,128)S(1)} %copy-done, bf16[256,256]{1,0:T(8,128)(2,1)S(1)} %get-tuple-element.17.weights.refs_2_), custom_call_target="tpu_custom_call" | custom-call | bytes 2555904 | tf_op jit(solution)/shard_map/lift_own/pallas_call | solution.py:427
  2.0 0.2 %collective-permute-done.refs_1_ = f32[32,32,128]{2,1,0:T(8,128)S(1)} collective-permute-done((f32[32,32,128]{2,1,0:T(8,128)}, f32[32,32,128]{2,1,0:T(8,128)S(1)}, u32[]{:S(2)}, u32[]{:S(2)}) %collective-permute-start) | collective-permute-done | bytes 524320 | tf_op jit(solution)/shard_map/ppermute | solution.py:449
  2.2 1.1 %make_messages.1 = (f32[39,64,128]{2,1,0:T(8,128)S(1)}, f32[32,32,128]{2,1,0:T(8,128)S(1)}, f32[16,16,128]{2,1,0:T(8,128)S(1)}, f32[8,8,128]{2,1,0:T(8,128)S(1)}...) custom-call(f32[39,64,128]{2,1,0:T(8,128)S(1)} %lift_own.1.refs_0_, ...), custom_call_target="tpu_custom_call", output_to_operand_aliasing={{0}: (0, {})} | custom-call | bytes 4218880 | tf_op jit(solution)/shard_map/make_messages/pallas_call | solution.py:427
  3.3 2.9 %collective-permute-start.1 = (f32[112,128]{1,0:T(8,128)S(1)}, f32[112,128]{1,0:T(8,128)S(1)}, u32[]{:S(2)}, u32[]{:S(2)}) collective-permute-start(f32[112,128]{1,0:T(8,128)S(1)} %get-tuple-element.24), channel_id=1, source_target_pairs={{0,2},{2,4},{4,6},{6,8},{8,10},{10,12},{12,14},{14,16},{16,18},{18... | collective-permute-start | bytes 172040 | tf_op jit(solution)/shard_map/ppermute | solution.py:536
  6.2 1.5 %collective-permute-start.2 = (f32[16,128]{1,0:T(8,128)S(1)}, f32[16,128]{1,0:T(8,128)S(1)}, u32[]{:S(2)}, u32[]{:S(2)}) collective-permute-start(f32[16,128]{1,0:T(8,128)S(1)} %get-tuple-element.25), channel_id=1, source_target_pairs={{0,4},{2,6},{4,8},{6,10},{8,12},{10,14},{12,16},{14,18},{16,20},{1... | collective-permute-start | bytes 24584 | tf_op jit(solution)/shard_map/ppermute | solution.py:536
  7.7 3.2 %collective-permute-start.3 = (f32[8,128]{1,0:T(8,128)S(1)}, f32[8,128]{1,0:T(8,128)S(1)}, u32[]{:S(2)}, u32[]{:S(2)}) collective-permute-start(f32[8,128]{1,0:T(8,128)S(1)} %get-tuple-element.26), channel_id=1, source_target_pairs={{0,28},{2,30},{4,0},{6,2},{8,4},{10,6},{12,8},{14,10},{16,12},{18,... | collective-permute-start | bytes 12296 | tf_op jit(solution)/shard_map/ppermute | solution.py:536
  10.9 1.4 %collective-permute-start.4 = (f32[128,128]{1,0:T(8,128)S(1)}, f32[128,128]{1,0:T(8,128)S(1)}, u32[]{:S(2)}, u32[]{:S(2)}) collective-permute-start(f32[128,128]{1,0:T(8,128)S(1)} %get-tuple-element.27), channel_id=1, source_target_pairs={{0,30},{2,0},{4,2},{6,4},{8,6},{10,8},{12,10},{14,12},{16,14},{18,... | collective-permute-start | bytes 196616 | tf_op jit(solution)/shard_map/ppermute | solution.py:536
  12.3 0.2 %finish_own.1._ = f32[32,32,128]{2,1,0:T(8,128)S(1)} custom-call(f32[39,64,128]{2,1,0:T(8,128)S(1)} %get-tuple-element.19.first, f32[32,32,128]{2,1,0:T(8,128)S(1)} %get-tuple-element.20._, f32[16,16,128]{2,1,0:T(8,128)S(1)} %get-tuple-element.21.refs_0_, f32[8,8,128]{2,1,0:T(8,128)S(1)} %get-tuple-element.22.refs_1_, ...), custom_call_target="tpu_custom_call", output_to_operand_aliasing={{}: (1, {})} | custom-call | bytes 1048576 | tf_op jit(solution)/shard_map/finish_own/pallas_call | solution.py:427
  12.5 0.3 %collective-permute-done.2.refs_1_ = f32[16,128]{1,0:T(8,128)S(1)} collective-permute-done((f32[16,128]{1,0:T(8,128)S(1)}, f32[16,128]{1,0:T(8,128)S(1)}, u32[]{:S(2)}, u32[]{:S(2)}) %collective-permute-start.2) | collective-permute-done | bytes 8224 | tf_op jit(solution)/shard_map/ppermute | solution.py:536
  12.7 0.0 collective-permute-done.1.refs_0_
  12.7 0.1 add_right.1._
  12.8 0.0 collective-permute-done.3.refs_0_
  12.8 2.4 %collective-permute-done.4.refs_1_ = f32[128,128]{1,0:T(8,128)S(1)} collective-permute-done((f32[128,128]{1,0:T(8,128)S(1)}, f32[128,128]{1,0:T(8,128)S(1)}, u32[]{:S(2)}, u32[]{:S(2)}) %collective-permute-start.4) | collective-permute-done | bytes 65568 | tf_op jit(solution)/shard_map/ppermute | solution.py:536
  15.2 0.9 %add_left.1 = (f32[32,32,128]{2,1,0:T(8,128)}, f32[32,32,128]{2,1,0:T(8,128)S(1)}) custom-call(f32[32,32,128]{2,1,0:T(8,128)S(1)} %add_right.1._, f32[8,128]{1,0:T(8,128)S(1)} %collective-permute-done.3.refs_0_, f32[128,128]{1,0:T(8,128)S(1)} %collective-permute-done.4.refs_1_), custom_call_target="tpu_custom_call", output_to_operand_aliasing={{1}: (0, {})} | custom-call | bytes 2097152 | tf_op jit(solution)/shard_map/add_left/pallas_call | solution.py:427
Async XLA Ops:
  0.0 1.6 %copy-start = (f32[32,32,128]{2,1,0:T(8,128)S(1)}, f32[32,32,128]{2,1,0:T(8,128)}, u32[]{:S(2)}) copy-start(f32[32,32,128]{2,1,0:T(8,128)} %velocity.1) | copy-start | bytes 1572868
  0.0 2.2 %collective-permute-start = (f32[32,32,128]{2,1,0:T(8,128)}, f32[32,32,128]{2,1,0:T(8,128)S(1)}, u32[]{:S(2)}, u32[]{:S(2)}) collective-permute-start(f32[32,32,128]{2,1,0:T(8,128)} %velocity.1), channel_id=1, source_target_pairs={{0,1},{1,0},{2,3},{3,2},{4,5},{5,4},{6,7},{7,6},{8,9},{9,8},{10,11... | collective-permute-start | bytes 1572872 | tf_op jit(solution)/shard_map/ppermute | solution.py:449
  3.3 9.4 %collective-permute-start.1 = (f32[112,128]{1,0:T(8,128)S(1)}, f32[112,128]{1,0:T(8,128)S(1)}, u32[]{:S(2)}, u32[]{:S(2)}) collective-permute-start(f32[112,128]{1,0:T(8,128)S(1)} %get-tuple-element.24), channel_id=1, source_target_pairs={{0,2},{2,4},{4,6},{6,8},{8,10},{10,12},{12,14},{14,16},{16,18},{18... | collective-permute-start | bytes 172040 | tf_op jit(solution)/shard_map/ppermute | solution.py:536
  6.2 6.5 %collective-permute-start.2 = (f32[16,128]{1,0:T(8,128)S(1)}, f32[16,128]{1,0:T(8,128)S(1)}, u32[]{:S(2)}, u32[]{:S(2)}) collective-permute-start(f32[16,128]{1,0:T(8,128)S(1)} %get-tuple-element.25), channel_id=1, source_target_pairs={{0,4},{2,6},{4,8},{6,10},{8,12},{10,14},{12,16},{14,18},{16,20},{1... | collective-permute-start | bytes 24584 | tf_op jit(solution)/shard_map/ppermute | solution.py:536
  7.7 5.1 %collective-permute-start.3 = (f32[8,128]{1,0:T(8,128)S(1)}, f32[8,128]{1,0:T(8,128)S(1)}, u32[]{:S(2)}, u32[]{:S(2)}) collective-permute-start(f32[8,128]{1,0:T(8,128)S(1)} %get-tuple-element.26), channel_id=1, source_target_pairs={{0,28},{2,30},{4,0},{6,2},{8,4},{10,6},{12,8},{14,10},{16,12},{18,... | collective-permute-start | bytes 12296 | tf_op jit(solution)/shard_map/ppermute | solution.py:536
  10.9 4.3 %collective-permute-start.4 = (f32[128,128]{1,0:T(8,128)S(1)}, f32[128,128]{1,0:T(8,128)S(1)}, u32[]{:S(2)}, u32[]{:S(2)}) collective-permute-start(f32[128,128]{1,0:T(8,128)S(1)} %get-tuple-element.27), channel_id=1, source_target_pairs={{0,30},{2,0},{4,2},{6,4},{8,6},{10,8},{12,10},{14,12},{16,14},{18,... | collective-permute-start | bytes 196616 | tf_op jit(solution)/shard_map/ppermute | solution.py:536
where the time goes:
time: 16.3 us; the launch traced here: 16.1 us
  starting transfers between devices  9.45 us (58%)
  Pallas kernels  3.79 us (23%)
  waiting for transfers between devices  2.82 us (17%)
    ppermute x4, starting transfers between devices, local(): lax.ppermute(sent[to], 'gx', [(i, (i + to) % around) for i in range(aroun...  9 us
    pallas_call x6, Pallas kernels, call(): pl.pallas_call(body, out_shape=shapes, in_specs=[vmem] * len(ins), out_sp...  3.79 us
    ppermute x4, waiting for transfers between devices, local(): lax.ppermute(sent[to], 'gx', [(i, (i + to) % around) for i in range(aroun...  2.62 us
    ppermute x1, starting transfers between devices, local(): lax.ppermute(velocity, 'gy', [(i, (i - k) % count) for i in range(count)])  0.45 us
  transfers between devices with their start and end apart: 5, of which 3 were waited for; matrix products, arithmetic and copies ran while one was open for 0% of the time, Pallas kernels for 11%

commit v1 on v0

--- a/solution.py
+++ b/solution.py
@@ -14,7 +14,8 @@
 VMEM_BYTES = 24 * 2**20
 FIRST_FLOPS = 10**10
 COPIES = 2
-SHARED = False
+SHARED = True
+SIDES = (1, -1)
 
 
 def windows(block):
@@ -302,7 +303,7 @@
                 messages[to][row : row + 1, :] = jnp.zeros((1, width), jnp.float32)
     if shared:
         for far, target in enumerate(passed, 1):
-            target[...] = jnp.where(lax.axis_index("gy") == 0, messages[-far][...], messages[far][...])
+            target[...] = jnp.where(lax.axis_index("gy") == 0, messages[far][...], messages[-far][...])
 
 
 def rest_kernel(block, rows, width, first, _, *refs):
@@ -394,7 +395,7 @@
 
 
 def keep_kernel(block, rows, _, near, far, out, *clean):
-    for core, side in enumerate((-1, 1)):
+    for core, side in enumerate(SIDES):
 
         @pl.when(lax.axis_index("gy") == core)
         def _():
@@ -409,7 +410,7 @@
 
 
 def swap_kernel(block, rows, one, _, packed, whole, out, done, *clean):
-    for core, side in enumerate((1, -1)):
+    for core, side in enumerate(SIDES[::-1]):
 
         @pl.when(lax.axis_index("gy") == core)
         def _():
@@ -504,7 +505,7 @@
                 [
                     (2 * i + core, 2 * ((i + side * step) % around) + core)
                     for i in range(around)
-                    for core, side in enumerate((-1, 1))
+                    for core, side in enumerate(SIDES)
                 ],
             )
             for step, value in enumerate(messages, 1)

time: 16.3 us -> 15.8 us (0.969)
  starting transfers between devices: 9.45 us -> 4.89 us
  waiting for transfers between devices: 2.82 us -> 6.84 us
    ppermute x4 -> x3, starting transfers between devices: 9 us -> 4.43 us  [the longest x2 4.43 us: local(): lax.ppermute(value, ('gx', 'gy'), [(2 * i + core, 2 * ((i + side * step)...]
    ppermute x4 -> x3, waiting for transfers between devices: 2.62 us -> 6.64 us  [the longest x2 5.67 us: local(): lax.ppermute(value, ('gx', 'gy'), [(2 * i + core, 2 * ((i + side * step)...]
    pallas_call x6 -> x7, Pallas kernels: 3.79 us -> 3.86 us  [call(): pl.pallas_call(body, out_shape=shapes, in_specs=[vmem] * len(ins), out_sp...]
  transfers between devices with their start and end apart: 5 -> 4, of which waited for: 3 -> 4; matrix products, arithmetic and copies ran while one was open for 0% -> 0% of each run, Pallas kernels for 11% -> 12%
where the time goes in v1:
time: 15.8 us; the launch traced here: 15.6 us
  waiting for transfers between devices  6.84 us (43%)
  starting transfers between devices  4.89 us (31%)
  Pallas kernels  3.86 us (24%)
    ppermute x2, waiting for transfers between devices, local(): lax.ppermute(value, ('gx', 'gy'), [(2 * i + core, 2 * ((i + side * step)...  5.67 us
    ppermute x2, starting transfers between devices, local(): lax.ppermute(value, ('gx', 'gy'), [(2 * i + core, 2 * ((i + side * step)...  4.43 us
    pallas_call x7, Pallas kernels, call(): pl.pallas_call(body, out_shape=shapes, in_specs=[vmem] * len(ins), out_sp...  3.86 us
    ppermute x1, waiting for transfers between devices, local(): packed = lax.ppermute(packed, 'gy', [(0, 1), (1, 0)])  0.97 us
    ppermute x1, starting transfers between devices, local(): lax.ppermute(velocity, 'gy', [(i, (i - k) % count) for i in range(count)])  0.45 us
  transfers between devices with their start and end apart: 4, of which 4 were waited for; matrix products, arithmetic and copies ran while one was open for 0% of the time, Pallas kernels for 12%

profile of v1, /device:TPU:0, one launch (start us, length us, event | category | flops | bytes accessed | tf_op | source)
XLA Modules:
  0.0 15.6 jit_solution(6860336685311351898)
XLA Ops:
  0.0 0.0 copy-start
  0.0 0.5 %collective-permute-start = (f32[32,32,128]{2,1,0:T(8,128)}, f32[32,32,128]{2,1,0:T(8,128)S(1)}, u32[]{:S(2)}, u32[]{:S(2)}) collective-permute-start(f32[32,32,128]{2,1,0:T(8,128)} %velocity.1), channel_id=1, source_target_pairs={{0,1},{1,0},{2,3},{3,2},{4,5},{5,4},{6,7},{7,6},{8,9},{9,8},{10,11... | collective-permute-start | bytes 1572872 | tf_op jit(solution)/shard_map/ppermute | solution.py:450
  0.5 1.2 %make_matrices.1 = (bf16[256,256]{1,0:T(8,128)(2,1)S(1)}, bf16[256,256]{1,0:T(8,128)(2,1)S(1)}) custom-call(), custom_call_target="tpu_custom_call" | custom-call | flops 10000000000 | bytes 1048576 | tf_op jit(solution)/shard_map/make_matrices/pallas_call | solution.py:428
  1.6 0.0 copy-done
  1.7 0.3 %lift_own.1.refs_0_ = f32[39,64,128]{2,1,0:T(8,128)S(1)} custom-call(f32[32,32,128]{2,1,0:T(8,128)S(1)} %copy-done, bf16[256,256]{1,0:T(8,128)(2,1)S(1)} %get-tuple-element.15.weights.refs_2_), custom_call_target="tpu_custom_call" | custom-call | bytes 2555904 | tf_op jit(solution)/shard_map/lift_own/pallas_call | solution.py:428
  2.0 0.2 %collective-permute-done.refs_1_ = f32[32,32,128]{2,1,0:T(8,128)S(1)} collective-permute-done((f32[32,32,128]{2,1,0:T(8,128)}, f32[32,32,128]{2,1,0:T(8,128)S(1)}, u32[]{:S(2)}, u32[]{:S(2)}) %collective-permute-start) | collective-permute-done | bytes 524320 | tf_op jit(solution)/shard_map/ppermute | solution.py:450
  2.2 1.2 %make_messages.1 = (f32[39,64,128]{2,1,0:T(8,128)S(1)}, f32[32,32,128]{2,1,0:T(8,128)S(1)}, f32[16,16,128]{2,1,0:T(8,128)S(1)}, f32[8,8,128]{2,1,0:T(8,128)S(1)}...) custom-call(f32[39,64,128]{2,1,0:T(8,128)S(1)} %lift_own.1.refs_0_, ...), custom_call_target="tpu_custom_call", output_to_operand_aliasing={{0}: (0, {})} | custom-call | bytes 4243456 | tf_op jit(solution)/shard_map/make_messages/pallas_call | solution.py:428
  3.4 2.9 %collective-permute-start.1 = (f32[256,128]{1,0:T(8,128)S(1)}, f32[256,128]{1,0:T(8,128)S(1)}, u32[]{:S(2)}, u32[]{:S(2)}) collective-permute-start(f32[256,128]{1,0:T(8,128)S(1)} %get-tuple-element.22), channel_id=1, source_target_pairs={{0,2},{1,31},{2,4},{3,1},{4,6},{5,3},{6,8},{7,5},{8,10},{9,7},{10,... | collective-permute-start | bytes 393224 | tf_op jit(solution)/shard_map/ppermute | solution.py:502
  6.3 1.5 %collective-permute-start.2 = (f32[32,128]{1,0:T(8,128)S(1)}, f32[32,128]{1,0:T(8,128)S(1)}, u32[]{:S(2)}, u32[]{:S(2)}) collective-permute-start(f32[32,128]{1,0:T(8,128)S(1)} %get-tuple-element.23), channel_id=1, source_target_pairs={{0,4},{1,29},{2,6},{3,31},{4,8},{5,1},{6,10},{7,3},{8,12},{9,5},{1... | collective-permute-start | bytes 49160 | tf_op jit(solution)/shard_map/ppermute | solution.py:502
  7.8 5.1 %collective-permute-done.2.far = f32[32,128]{1,0:T(8,128)S(1)} collective-permute-done((f32[32,128]{1,0:T(8,128)S(1)}, f32[32,128]{1,0:T(8,128)S(1)}, u32[]{:S(2)}, u32[]{:S(2)}) %collective-permute-start.2) | collective-permute-done | bytes 16416 | tf_op jit(solution)/shard_map/ppermute | solution.py:502
  12.9 0.6 %collective-permute-done.1.near = f32[256,128]{1,0:T(8,128)S(1)} collective-permute-done((f32[256,128]{1,0:T(8,128)S(1)}, f32[256,128]{1,0:T(8,128)S(1)}, u32[]{:S(2)}, u32[]{:S(2)}) %collective-permute-start.1) | collective-permute-done | bytes 131104 | tf_op jit(solution)/shard_map/ppermute | solution.py:502
  13.5 0.0 collective-permute-start.3
  13.5 0.2 %finish_own.1._ = f32[32,32,128]{2,1,0:T(8,128)S(1)} custom-call(f32[39,64,128]{2,1,0:T(8,128)S(1)} %get-tuple-element.17.first, f32[32,32,128]{2,1,0:T(8,128)S(1)} %get-tuple-element.18._, f32[16,16,128]{2,1,0:T(8,128)S(1)} %get-tuple-element.19.refs_0_, f32[8,8,128]{2,1,0:T(8,128)S(1)} %get-tuple-element.20.refs_1_, ...), custom_call_target="tpu_custom_call", output_to_operand_aliasing={{}: (1, {})} | custom-call | bytes 1048576 | tf_op jit(solution)/shard_map/finish_own/pallas_call | solution.py:428
  13.7 0.1 add_kept.1._
  13.8 1.0 %collective-permute-done.3.packed = f32[144,128]{1,0:T(8,128)S(1)} collective-permute-done((f32[144,128]{1,0:T(8,128)S(1)}, f32[144,128]{1,0:T(8,128)S(1)}, u32[]{:S(2)}, u32[]{:S(2)}) %collective-permute-start.3) | collective-permute-done | bytes 73760 | tf_op jit(solution)/shard_map/ppermute | solution.py:515
  14.7 0.9 %add_swapped.1 = (f32[32,32,128]{2,1,0:T(8,128)}, f32[32,32,128]{2,1,0:T(8,128)S(1)}) custom-call(f32[32,32,128]{2,1,0:T(8,128)S(1)} %add_kept.1._, f32[144,128]{1,0:T(8,128)S(1)} %collective-permute-done.3.packed), custom_call_target="tpu_custom_call", output_to_operand_aliasing={{1}: (0, {})} | custom-call | bytes 2097152 | tf_op jit(solution)/shard_map/add_swapped/pallas_call | solution.py:428
  (1 shorter events, 0.0 us)
Async XLA Ops:
  0.0 1.6 %copy-start = (f32[32,32,128]{2,1,0:T(8,128)S(1)}, f32[32,32,128]{2,1,0:T(8,128)}, u32[]{:S(2)}) copy-start(f32[32,32,128]{2,1,0:T(8,128)} %velocity.1) | copy-start | bytes 1572868
  0.0 2.2 %collective-permute-start = (f32[32,32,128]{2,1,0:T(8,128)}, f32[32,32,128]{2,1,0:T(8,128)S(1)}, u32[]{:S(2)}, u32[]{:S(2)}) collective-permute-start(f32[32,32,128]{2,1,0:T(8,128)} %velocity.1), channel_id=1, source_target_pairs={{0,1},{1,0},{2,3},{3,2},{4,5},{5,4},{6,7},{7,6},{8,9},{9,8},{10,11... | collective-permute-start | bytes 1572872 | tf_op jit(solution)/shard_map/ppermute | solution.py:450
  3.4 10.1 %collective-permute-start.1 = (f32[256,128]{1,0:T(8,128)S(1)}, f32[256,128]{1,0:T(8,128)S(1)}, u32[]{:S(2)}, u32[]{:S(2)}) collective-permute-start(f32[256,128]{1,0:T(8,128)S(1)} %get-tuple-element.22), channel_id=1, source_target_pairs={{0,2},{1,31},{2,4},{3,1},{4,6},{5,3},{6,8},{7,5},{8,10},{9,7},{10,... | collective-permute-start | bytes 393224 | tf_op jit(solution)/shard_map/ppermute | solution.py:502
  6.3 6.6 %collective-permute-start.2 = (f32[32,128]{1,0:T(8,128)S(1)}, f32[32,128]{1,0:T(8,128)S(1)}, u32[]{:S(2)}, u32[]{:S(2)}) collective-permute-start(f32[32,128]{1,0:T(8,128)S(1)} %get-tuple-element.23), channel_id=1, source_target_pairs={{0,4},{1,29},{2,6},{3,31},{4,8},{5,1},{6,10},{7,3},{8,12},{9,5},{1... | collective-permute-start | bytes 49160 | tf_op jit(solution)/shard_map/ppermute | solution.py:502
  13.5 1.3 %collective-permute-start.3 = (f32[144,128]{1,0:T(8,128)S(1)}, f32[144,128]{1,0:T(8,128)S(1)}, u32[]{:S(2)}, u32[]{:S(2)}) collective-permute-start(f32[144,128]{1,0:T(8,128)S(1)} %pack_other.1), channel_id=1, source_target_pairs={{0,1},{1,0},{2,3},{3,2},{4,5},{5,4},{6,7},{7,6},{8,9},{9,8},{10,11... | collective-permute-start | bytes 221192 | tf_op jit(solution)/shard_map/ppermute | solution.py:515

commit v2 on v1

--- a/solution.py
+++ b/solution.py
@@ -13,7 +13,6 @@
 SCALE = 1.149604398
 VMEM_BYTES = 24 * 2**20
 FIRST_FLOPS = 10**10
-COPIES = 2
 SHARED = True
 SIDES = (1, -1)
 
@@ -45,11 +44,18 @@
                 derived[level, edge + 2 * sign] = (far, None)
             if far in planes and near in planes:
                 derived[level, edge] = (far, near)
+        planes = [plane for plane in planes if (level, plane) not in derived]
         at = base
+        if level == 1:
+            extra = planes[-1] if len(planes) > 3 else None
+        elif level > 1 and extra is not None:
+            at = base + (rows >> 1)
         for plane in planes:
-            if (level, plane) not in derived:
-                sent[level, plane] = at
-                at += height
+            if level == 1 and plane == extra:
+                sent[level, plane] = base, shift_of(2)
+                continue
+            sent[level, plane] = at, shift_of(level)
+            at += height
         ends = max(ends, at)
         if level == 0:
             base = at
@@ -231,7 +237,10 @@
             own[level][plane, pl.ds(0, number, 2), :] = even
             own[level][plane, pl.ds(1, number, 2), :] = odd
         else:
-            at = tables[to][0][level, plane] + half * lengths[to]
+            at, shift = tables[to][0][level, plane]
+            at += half * lengths[to]
+            if shift != shift_of(level):
+                even, odd = (pltpu.roll(value, shift - shift_of(level), 1) for value in (even, odd))
             post(to, at, number, even)
             post(to, at + 1, number, odd)
 
@@ -329,33 +338,35 @@
     sent, derived, _ = message(block, rows, to)
     a, b, c, d = STEPS
     width = out.shape[-1]
+    lane = lax.broadcasted_iota(jnp.int32, (1, width), 1)
     for level in sorted({level for level, _ in sent}):
         spacing, height = 1 << level, rows >> level
         shape = (height, width)
-        if level > 0:
-            here = [at for (found, _), at in sent.items() if found == level]
-            start, stop = min(here), -(-(max(here) + height) // 8) * 8
-            value = arrived[base + start : base + stop, :]
-            if shift_of(level):
-                value = pltpu.roll(value, width - shift_of(level), 1)
-            lane = lax.broadcasted_iota(jnp.int32, (1, width), 1)
-            value = jnp.where(lax.rem(lane, spacing) == 0, value, 0.0)
-            source = clean[level - 1]
-            source[: stop - start, :] = value
-        else:
-            start, source = -base, arrived
+        held = {}
+        for shift in sorted({shift for (found, _), (_, shift) in sent.items() if found == level}):
+            here = {
+                plane: at for (found, plane), (at, by) in sent.items() if (found, by) == (level, shift)
+            }
+            start, stop = min(here.values()), -(-(max(here.values()) + height) // 8) * 8
+            source, offset = arrived, base
+            if level > 0:
+                value = arrived[base + start : base + stop, :]
+                if shift:
+                    value = pltpu.roll(value, width - shift, 1)
+                source, offset = clean[level if shift == shift_of(level) else 0], -start
+                source[: stop - start, :] = jnp.where(lax.rem(lane, spacing) == 0, value, 0.0)
+            held |= {plane: (source, at + offset) for plane, at in here.items()}
 
         def read(plane):
-            at = sent[level, plane] - start
+            source, at = held[plane]
             return source[at : at + height, :]
 
         def add(plane, value):
             x = (plane - to * (block >> level)) * spacing
             out[x, pl.ds(0, height, spacing), :] += value
 
-        for found, plane in sent:
-            if found == level:
-                add(plane, read(plane))
+        for plane in held:
+            add(plane, read(plane))
         for (found, plane), (far, near) in derived.items():
             if found == level:
                 if near is None:
@@ -367,14 +378,26 @@
                 add(plane, jnp.where(keep, value, 0.0))
 
 
-def write_out(out, whole, done):
-    parts = done.shape[0]
-    size = out.shape[0] // parts
+def touched(block, rows, side):
+    found = set()
+    for to in (side, 2 * side):
+        sent, derived, _ = message(block, rows, to)
+        found |= {(plane - to * (block >> level)) << level for level, plane in [*sent, *derived]}
+    runs = []
+    for x in sorted(found):
+        if runs and x - runs[-1][1] <= 1:
+            runs[-1] = (runs[-1][0], x + 1)
+        else:
+            runs.append((x, x + 1))
+    return runs
+
+
+def write_out(out, whole, done, runs):
     copies = [
         pltpu.make_async_copy(
-            out.at[pl.ds(part * size, size)], whole.at[pl.ds(part * size, size)], done.at[part]
+            out.at[pl.ds(start, stop - start)], whole.at[pl.ds(start, stop - start)], done.at[n]
         )
-        for part in range(parts)
+        for n, (start, stop) in enumerate(runs)
     ]
     for copy in copies:
         copy.start()
@@ -391,10 +414,10 @@
     for to, arrived in zip(places, received):
         add_message(block, rows, to, arrived, 0, out, clean)
     if last:
-        write_out(out, whole, done)
-
-
-def keep_kernel(block, rows, _, near, far, out, *clean):
+        write_out(out, whole, done, [(0, block)])
+
+
+def keep_kernel(block, rows, _, near, far, whole, out, done, *clean):
     for core, side in enumerate(SIDES):
 
         @pl.when(lax.axis_index("gy") == core)
@@ -402,6 +425,8 @@
             add_message(block, rows, side, near, 0, out, clean)
             add_message(block, rows, 2 * side, far, 0, out, clean)
 
+    write_out(out, whole, done, [(0, block)])
+
 
 def pack_kernel(near, far, packed):
     one, two = near.shape[0] // 2, far.shape[0] // 2
@@ -409,18 +434,17 @@
     packed[one:, :] = far[two:, :]
 
 
-def swap_kernel(block, rows, one, _, packed, whole, out, done, *clean):
+def swap_kernel(block, rows, one, own, packed, before, whole, out, done, *clean):
     for core, side in enumerate(SIDES[::-1]):
 
         @pl.when(lax.axis_index("gy") == core)
         def _():
             add_message(block, rows, side, packed, 0, out, clean)
             add_message(block, rows, 2 * side, packed, one, out, clean)
-
-    write_out(out, whole, done)
-
-
-def call(body, name, outs, ins, scratch=(), aliases=None, flops=0, hbm_out=()):
+            write_out(out, whole, done, touched(block, rows, side))
+
+
+def call(body, name, outs, ins, scratch=(), aliases=None, flops=0, hbm_out=(), hbm_in=()):
     vmem, hbm = pl.BlockSpec(memory_space=pltpu.VMEM), pl.BlockSpec(memory_space=pltpu.HBM)
     f32 = jnp.float32
     shapes = [out if isinstance(out, jax.ShapeDtypeStruct) else jax.ShapeDtypeStruct(out, f32) for out in outs]
@@ -428,7 +452,7 @@
     return pl.pallas_call(
         body,
         out_shape=shapes,
-        in_specs=[vmem] * len(ins),
+        in_specs=[hbm if n in hbm_in else vmem for n in range(len(ins))],
         out_specs=[hbm if n in hbm_out else vmem for n in range(len(outs))],
         scratch_shapes=[pltpu.VMEM(shape, f32) if isinstance(shape, tuple) else shape for shape in scratch],
         input_output_aliases=aliases or {},
@@ -461,7 +485,7 @@
     owned = [(block >> level, rows >> level, width) for level in range(LEVELS)]
     lengths = {to: message(block, rows, to)[2] for to in places}
     one, two = max(lengths[1], lengths[-1]), max(lengths[2], lengths[-2])
-    clean = [(one, width)] * (LEVELS - 1)
+    clean = [(one, width)] * LEVELS
 
     square = jax.ShapeDtypeStruct((2 * width, 2 * width), jnp.bfloat16)
     weights = call(matrix_kernel, "make_matrices", [square] * 2, [], flops=FIRST_FLOPS)
@@ -496,7 +520,7 @@
             aliases={1: 0},
         )[0]
 
-    written = [pltpu.SemaphoreType.DMA((COPIES,))]
+    written = [pltpu.SemaphoreType.DMA((block,))]
     if shared:
         near, far = (
             lax.ppermute(
@@ -513,22 +537,24 @@
         result = rest()
         (packed,) = call(pack_kernel, "pack_other", [(one + two, width)], [near, far])
         packed = lax.ppermute(packed, "gy", [(0, 1), (1, 0)])
-        (result,) = call(
+        whole, result = call(
             functools.partial(keep_kernel, block, rows),
             "add_kept",
-            [owned[0]],
+            [owned[0]] * 2,
             [result, near, far],
-            clean,
-            aliases={0: 0},
+            written + clean,
+            aliases={0: 1},
+            hbm_out=(0,),
         )
         whole, _ = call(
             functools.partial(swap_kernel, block, rows, one),
             "add_swapped",
             [owned[0]] * 2,
-            [result, packed],
+            [result, packed, whole],
             written + clean,
-            aliases={0: 1},
+            aliases={0: 1, 2: 0},
             hbm_out=(0,),
+            hbm_in=(2,),
         )
         return whole
 

time: 15.8 us -> 15.9 us (level)
  Pallas kernels: 3.86 us -> 5.12 us
  waiting for transfers between devices: 6.84 us -> 5.67 us
    pallas_call x7, Pallas kernels: 3.86 us -> 5.12 us  [call(): pl.pallas_call(body, out_shape=shapes, in_specs=[hbm if n in hbm_in else...]
    ppermute x1, waiting for transfers between devices: 0.97 us -> 0.01 us  [local(): packed = lax.ppermute(packed, 'gy', [(0, 1), (1, 0)])]
    ppermute x2, waiting for transfers between devices: 5.67 us -> 5.47 us  [local(): lax.ppermute(value, ('gx', 'gy'), [(2 * i + core, 2 * ((i + side * step)...]
  transfers between devices with their start and end apart: 4 -> 4, of which waited for: 4 -> 3; matrix products, arithmetic and copies ran while one was open for 0% -> 0% of each run, Pallas kernels for 12% -> 18%
where the time goes in v2:
time: 15.9 us; the launch traced here: 15.7 us
  waiting for transfers between devices  5.67 us (36%)
  Pallas kernels  5.12 us (32%)
  starting transfers between devices  4.9 us (31%)
    ppermute x2, waiting for transfers between devices, local(): lax.ppermute(value, ('gx', 'gy'), [(2 * i + core, 2 * ((i + side * step)...  5.47 us
    pallas_call x7, Pallas kernels, call(): pl.pallas_call(body, out_shape=shapes, in_specs=[hbm if n in hbm_in else...  5.12 us
    ppermute x2, starting transfers between devices, local(): lax.ppermute(value, ('gx', 'gy'), [(2 * i + core, 2 * ((i + side * step)...  4.43 us
    ppermute x1, starting transfers between devices, local(): lax.ppermute(velocity, 'gy', [(i, (i - k) % count) for i in range(count)])  0.45 us
  transfers between devices with their start and end apart: 4, of which 3 were waited for; matrix products, arithmetic and copies ran while one was open for 0% of the time, Pallas kernels for 18%

profile of v2, /device:TPU:0, one launch (start us, length us, event | category | flops | bytes accessed | tf_op | source)
XLA Modules:
  0.0 15.7 jit_solution(9144741631001908859)
XLA Ops:
  0.0 0.0 copy-start
  0.0 0.5 %collective-permute-start = (f32[32,32,128]{2,1,0:T(8,128)}, f32[32,32,128]{2,1,0:T(8,128)S(1)}, u32[]{:S(2)}, u32[]{:S(2)}) collective-permute-start(f32[32,32,128]{2,1,0:T(8,128)} %velocity.1), channel_id=1, source_target_pairs={{0,1},{1,0},{2,3},{3,2},{4,5},{5,4},{6,7},{7,6},{8,9},{9,8},{10,11... | collective-permute-start | bytes 1572872 | tf_op jit(solution)/shard_map/ppermute | solution.py:474
  0.5 1.2 %make_matrices.1 = (bf16[256,256]{1,0:T(8,128)(2,1)S(1)}, bf16[256,256]{1,0:T(8,128)(2,1)S(1)}) custom-call(), custom_call_target="tpu_custom_call" | custom-call | flops 10000000000 | bytes 1048576 | tf_op jit(solution)/shard_map/make_matrices/pallas_call | solution.py:452
  1.6 0.0 copy-done
  1.7 0.3 %lift_own.1.refs_0_ = f32[39,64,128]{2,1,0:T(8,128)S(1)} custom-call(f32[32,32,128]{2,1,0:T(8,128)S(1)} %copy-done, bf16[256,256]{1,0:T(8,128)(2,1)S(1)} %get-tuple-element.17.weights.refs_2_), custom_call_target="tpu_custom_call" | custom-call | bytes 2555904 | tf_op jit(solution)/shard_map/lift_own/pallas_call | solution.py:452
  2.0 0.2 %collective-permute-done.refs_1_ = f32[32,32,128]{2,1,0:T(8,128)S(1)} collective-permute-done((f32[32,32,128]{2,1,0:T(8,128)}, f32[32,32,128]{2,1,0:T(8,128)S(1)}, u32[]{:S(2)}, u32[]{:S(2)}) %collective-permute-start) | collective-permute-done | bytes 524320 | tf_op jit(solution)/shard_map/ppermute | solution.py:474
  2.2 1.2 %make_messages.1 = (f32[39,64,128]{2,1,0:T(8,128)S(1)}, f32[32,32,128]{2,1,0:T(8,128)S(1)}, f32[16,16,128]{2,1,0:T(8,128)S(1)}, f32[8,8,128]{2,1,0:T(8,128)S(1)}...) custom-call(f32[39,64,128]{2,1,0:T(8,128)S(1)} %lift_own.1.refs_0_, ...), custom_call_target="tpu_custom_call", output_to_operand_aliasing={{0}: (0, {})} | custom-call | bytes 4210688 | tf_op jit(solution)/shard_map/make_messages/pallas_call | solution.py:452
  3.4 2.9 %collective-permute-start.1 = (f32[224,128]{1,0:T(8,128)S(1)}, f32[224,128]{1,0:T(8,128)S(1)}, u32[]{:S(2)}, u32[]{:S(2)}) collective-permute-start(f32[224,128]{1,0:T(8,128)S(1)} %get-tuple-element.24), channel_id=1, source_target_pairs={{0,2},{1,31},{2,4},{3,1},{4,6},{5,3},{6,8},{7,5},{8,10},{9,7},{10,... | collective-permute-start | bytes 344072 | tf_op jit(solution)/shard_map/ppermute | solution.py:526
  6.3 1.5 %collective-permute-start.2 = (f32[32,128]{1,0:T(8,128)S(1)}, f32[32,128]{1,0:T(8,128)S(1)}, u32[]{:S(2)}, u32[]{:S(2)}) collective-permute-start(f32[32,128]{1,0:T(8,128)S(1)} %get-tuple-element.25), channel_id=1, source_target_pairs={{0,4},{1,29},{2,6},{3,31},{4,8},{5,1},{6,10},{7,3},{8,12},{9,5},{1... | collective-permute-start | bytes 49160 | tf_op jit(solution)/shard_map/ppermute | solution.py:526
  7.8 5.1 %collective-permute-done.2.far = f32[32,128]{1,0:T(8,128)S(1)} collective-permute-done((f32[32,128]{1,0:T(8,128)S(1)}, f32[32,128]{1,0:T(8,128)S(1)}, u32[]{:S(2)}, u32[]{:S(2)}) %collective-permute-start.2) | collective-permute-done | bytes 16416 | tf_op jit(solution)/shard_map/ppermute | solution.py:526
  12.9 0.4 %collective-permute-done.1.near = f32[224,128]{1,0:T(8,128)S(1)} collective-permute-done((f32[224,128]{1,0:T(8,128)S(1)}, f32[224,128]{1,0:T(8,128)S(1)}, u32[]{:S(2)}, u32[]{:S(2)}) %collective-permute-start.1) | collective-permute-done | bytes 114720 | tf_op jit(solution)/shard_map/ppermute | solution.py:526
  13.3 0.0 collective-permute-start.3
  13.3 0.2 %finish_own.1._ = f32[32,32,128]{2,1,0:T(8,128)S(1)} custom-call(f32[39,64,128]{2,1,0:T(8,128)S(1)} %get-tuple-element.19.first, f32[32,32,128]{2,1,0:T(8,128)S(1)} %get-tuple-element.20._, f32[16,16,128]{2,1,0:T(8,128)S(1)} %get-tuple-element.21.refs_0_, f32[8,8,128]{2,1,0:T(8,128)S(1)} %get-tuple-element.22.refs_1_, ...), custom_call_target="tpu_custom_call", output_to_operand_aliasing={{}: (1, {})} | custom-call | bytes 1048576 | tf_op jit(solution)/shard_map/finish_own/pallas_call | solution.py:452
  13.5 1.2 %add_kept.1 = (f32[32,32,128]{2,1,0:T(8,128)}, f32[32,32,128]{2,1,0:T(8,128)S(1)}) custom-call(f32[32,32,128]{2,1,0:T(8,128)S(1)} %finish_own.1._, f32[224,128]{1,0:T(8,128)S(1)} %collective-permute-done.1.near, f32[32,128]{1,0:T(8,128)S(1)} %collective-permute-done.2.far), custom_call_target="tpu_custom_call", output_to_operand_aliasing={{1}: (0, {})} | custom-call | bytes 2097152 | tf_op jit(solution)/shard_map/add_kept/pallas_call | solution.py:452
  14.6 0.0 collective-permute-done.3.packed
  14.7 1.1 %add_swapped.1 = (f32[32,32,128]{2,1,0:T(8,128)}, f32[32,32,128]{2,1,0:T(8,128)S(1)}) custom-call(f32[32,32,128]{2,1,0:T(8,128)S(1)} %get-tuple-element.26.own, f32[128,128]{1,0:T(8,128)S(1)} %collective-permute-done.3.packed, f32[32,32,128]{2,1,0:T(8,128)} %get-tuple-element.27.before), custom_call_target="tpu_custom_call", output_to_operand_aliasing={{1}: (0, {}), {0}: (2, {})} | custom-call | bytes 2097152 | tf_op jit(solution)/shard_map/add_swapped/pallas_call | solution.py:452
  (1 shorter events, 0.0 us)
Async XLA Ops:
  0.0 1.6 %copy-start = (f32[32,32,128]{2,1,0:T(8,128)S(1)}, f32[32,32,128]{2,1,0:T(8,128)}, u32[]{:S(2)}) copy-start(f32[32,32,128]{2,1,0:T(8,128)} %velocity.1) | copy-start | bytes 1572868
  0.0 2.2 %collective-permute-start = (f32[32,32,128]{2,1,0:T(8,128)}, f32[32,32,128]{2,1,0:T(8,128)S(1)}, u32[]{:S(2)}, u32[]{:S(2)}) collective-permute-start(f32[32,32,128]{2,1,0:T(8,128)} %velocity.1), channel_id=1, source_target_pairs={{0,1},{1,0},{2,3},{3,2},{4,5},{5,4},{6,7},{7,6},{8,9},{9,8},{10,11... | collective-permute-start | bytes 1572872 | tf_op jit(solution)/shard_map/ppermute | solution.py:474
  3.4 9.9 %collective-permute-start.1 = (f32[224,128]{1,0:T(8,128)S(1)}, f32[224,128]{1,0:T(8,128)S(1)}, u32[]{:S(2)}, u32[]{:S(2)}) collective-permute-start(f32[224,128]{1,0:T(8,128)S(1)} %get-tuple-element.24), channel_id=1, source_target_pairs={{0,2},{1,31},{2,4},{3,1},{4,6},{5,3},{6,8},{7,5},{8,10},{9,7},{10,... | collective-permute-start | bytes 344072 | tf_op jit(solution)/shard_map/ppermute | solution.py:526
  6.3 6.6 %collective-permute-start.2 = (f32[32,128]{1,0:T(8,128)S(1)}, f32[32,128]{1,0:T(8,128)S(1)}, u32[]{:S(2)}, u32[]{:S(2)}) collective-permute-start(f32[32,128]{1,0:T(8,128)S(1)} %get-tuple-element.25), channel_id=1, source_target_pairs={{0,4},{1,29},{2,6},{3,31},{4,8},{5,1},{6,10},{7,3},{8,12},{9,5},{1... | collective-permute-start | bytes 49160 | tf_op jit(solution)/shard_map/ppermute | solution.py:526
  13.3 1.4 %collective-permute-start.3 = (f32[128,128]{1,0:T(8,128)S(1)}, f32[128,128]{1,0:T(8,128)S(1)}, u32[]{:S(2)}, u32[]{:S(2)}) collective-permute-start(f32[128,128]{1,0:T(8,128)S(1)} %pack_other.1), channel_id=1, source_target_pairs={{0,1},{1,0},{2,3},{3,2},{4,5},{5,4},{6,7},{7,6},{8,9},{9,8},{10,11... | collective-permute-start | bytes 196616 | tf_op jit(solution)/shard_map/ppermute | solution.py:539
